TPU v7x, 32 devices: a whole 2x2x4 slice. The times are simulated.
32 devices in a mesh: row: 4 (over x, core), col: 8 (over z, y).
Axes of the slice: x: 2, y: 2, z: 4, core: 2. Of those that a mesh axis runs over, the one named last changes fastest.
Arguments:
- leaf_rhs: bfloat16 [768, 128, 512], P(('row', 'col')), may hold values from -6 to 6
- leaf_inverse: bfloat16 [768, 128, 128], P(('row', 'col')), as said below
- leaf_link: bfloat16 [768, 128, 128], P(('row', 'col')), may hold values from -0.109375 to 0.109375
- leaf_parent: int32 [768], P(('row', 'col')), may hold values from 0 to 31, as said below
- node_rhs: bfloat16 [32, 128, 512], P(('row', 'col')), may hold values from -6 to 6
- node_inverse: bfloat16 [32, 128, 128], P(('row', 'col')), as said below
- node_link: bfloat16 [32, 128, 128], P(('row', 'col')), may hold values from -0.5 to 0.5
- node_parent: int32 [32], P('row'), may hold values from 0 to 31, as said below
- middle_rhs: bfloat16 [32, 128, 512], P('row'), may hold values from -6 to 6
- middle_inverse: bfloat16 [32, 128, 128], P('row'), as said below
- middle_link: bfloat16 [32, 128, 128], P('row'), may hold values from -0.1875 to 0.1875
- middle_parent: int32 [32], P('row'), may hold values from 0 to 3
- top_rhs: bfloat16 [4, 128, 512], replicated, may hold values from -6 to 6
- top_inverse: bfloat16 [4, 128, 128], replicated, as said below
Outputs:
- leaf_result: bfloat16 [768, 128, 512], P(('row', 'col'))
- node_result: bfloat16 [32, 128, 512], P(('row', 'col'))
- middle_result: bfloat16 [32, 128, 512], P('row')
- top_result: bfloat16 [4, 128, 512], replicated
Inputs may be any that keep to these rules, and one draw needn't show every extreme that they name: `leaf_parent`: the parent of a leaf held by the device at grid row r lies in block row r: it is r * 8 + c for some c below 8. `node_parent`: the parent of second-level supernode r * 8 + c is r * 8 + j for some j below 8. `leaf_inverse`: each block is lower triangular. `node_inverse`: each block is lower triangular. `middle_inverse`: each block is lower triangular. `top_inverse`: each block is lower triangular.
All inputs are finite; a program needn't handle non-finite values.
Results may differ from a plain program's by a relative error of at most 0.017.
Values may be sent and summed in bfloat16 or wider, within the bound.
A program may use at most 128 MiB of HBM per device.

v0:
```python
import jax
import jax.numpy as jnp
from jax import lax
from jax.sharding import PartitionSpec as P


def apply_block(matrix, vectors):
    return jnp.einsum("nij,njr->nir", matrix, vectors, preferred_element_type=jnp.float32)


def apply_transposed(matrix, vectors):
    return jnp.einsum("nij,nir->njr", matrix, vectors, preferred_element_type=jnp.float32)


def slot_sums(targets, count, values):
    slots = lax.iota(jnp.int32, count)
    select = (slots[:, None] == targets[None, :]).astype(jnp.float32)
    return jnp.einsum("sk,kwr->swr", select, values, precision=lax.Precision.HIGHEST)


def local(
    leaf_rhs,
    leaf_inverse,
    leaf_link,
    leaf_parent,
    node_rhs,
    node_inverse,
    node_link,
    node_parent,
    middle_rhs,
    middle_inverse,
    middle_link,
    middle_parent,
    top_rhs,
    top_inverse,
):
    peers = lax.axis_size("col")
    col_index = lax.axis_index("col")
    middle_count = middle_rhs.shape[0]
    top_count = top_rhs.shape[0]
    leaf_target = leaf_parent % peers
    middle_target = node_parent % middle_count
    leaf_solved = apply_block(leaf_inverse, leaf_rhs).astype(jnp.bfloat16)
    leaf_update = apply_block(leaf_link, leaf_solved)
    node_sum = lax.psum_scatter(
        slot_sums(leaf_target, lax.axis_size("col") * 1, leaf_update),
        "col",
        scatter_dimension=0,
        tiled=True,
    )
    node_y = (node_rhs.astype(jnp.float32) - node_sum).astype(jnp.bfloat16)
    node_solved = apply_block(node_inverse, node_y).astype(jnp.bfloat16)
    own_target = lax.dynamic_slice_in_dim(middle_target, col_index, 1)
    middle_term = slot_sums(own_target, middle_count, apply_block(node_link, node_solved))
    middle_sum = lax.psum(middle_term, "col")
    middle_y = (middle_rhs.astype(jnp.float32) - middle_sum).astype(jnp.bfloat16)
    middle_solved = apply_block(middle_inverse, middle_y).astype(jnp.bfloat16)
    top_term = slot_sums(middle_parent, top_count, apply_block(middle_link, middle_solved))
    top_sum = lax.psum(top_term, "row")
    top_y = (top_rhs.astype(jnp.float32) - top_sum).astype(jnp.bfloat16)
    top_solved = apply_block(top_inverse, top_y).astype(jnp.bfloat16)
    top_result = apply_transposed(top_inverse, top_solved).astype(jnp.bfloat16)
    middle_w = (
        middle_solved.astype(jnp.float32) - apply_transposed(middle_link, top_result[middle_parent])
    ).astype(jnp.bfloat16)
    middle_result = apply_transposed(middle_inverse, middle_w).astype(jnp.bfloat16)
    node_w = (
        node_solved.astype(jnp.float32) - apply_transposed(node_link, middle_result[own_target])
    ).astype(jnp.bfloat16)
    node_result = apply_transposed(node_inverse, node_w).astype(jnp.bfloat16)
    row_result = lax.all_gather(node_result, "col", axis=0, tiled=True)
    leaf_w = (
        leaf_solved.astype(jnp.float32) - apply_transposed(leaf_link, row_result[leaf_target])
    ).astype(jnp.bfloat16)
    leaf_result = apply_transposed(leaf_inverse, leaf_w).astype(jnp.bfloat16)
    return (leaf_result, node_result, middle_result, top_result)


def solution(mesh):
    placed = (
        P(("row", "col"), None, None),
        P(("row", "col"), None, None),
        P(("row", "col"), None, None),
        P(("row", "col")),
        P(("row", "col"), None, None),
        P(("row", "col"), None, None),
        P(("row", "col"), None, None),
        P("row"),
        P("row", None, None),
        P("row", None, None),
        P("row", None, None),
        P("row"),
        P(),
        P(),
    )
    return jax.shard_map(
        local,
        mesh=mesh,
        in_specs=placed,
        out_specs=(
            P(("row", "col"), None, None),
            P(("row", "col"), None, None),
            P("row", None, None),
            P(),
        ),
        check_vma=False,
    )
```

profile of v0, /device:TPU:0, one launch (start us, length us, event | category | flops | bytes accessed | tf_op | source)
XLA Modules:
  0.0 333.2 jit_solution(11601962516745921794)
XLA Ops:
  7.2 0.0 copy-start
  7.2 0.0 reduce-scatter.2.cloned.1.call-start
  7.2 1.8 copy-done
  9.1 0.0 copy-start.3
  9.1 2.2 convolution_convert_fusion
  11.2 0.0 copy-start.1
  11.2 1.7 copy-done.1
  12.9 0.0 copy-done.3
  12.9 3.7 %convolution_bitcast_fusion = f32[24,128,512]{1,2,0:T(8,128)} fusion(bf16[24,128,512]{2,1,0:T(8,128)(2,1)S(1)} %convolution_convert_fusion, bf16[24,128,128]{2,1,0:T(8,128)(2,1)S(1)} %copy-done.3), kind=kOutput, calls=%fused_computation.7 | convolution fusion | flops 402653184 | bytes 10223616 | tf_op jit(solution)/shard_map/nij,njr->nir/dot_general | solution.py:8
  16.6 0.0 copy-start.7
  16.6 6.7 %copy.50 = f32[24,128,512]{2,0,1:T(8,128)} copy(f32[24,128,512]{1,2,0:T(8,128)} %convolution_bitcast_fusion) | data formatting | bytes 12582912 | tf_op jit(solution)/shard_map/nij,njr->nir/dot_general | solution.py:8
  23.3 0.0 copy-done.7
  23.3 5.5 %fusion.22 = f32[8,128,512]{2,0,1:T(8,128)S(1)} fusion(f32[24,128,512]{2,0,1:T(8,128)} %copy.50, s32[24]{0:T(128)S(1)} %get-tuple-element.32), kind=kOutput, calls=%fused_computation.37 | convolution fusion | flops 150995136 | bytes 8388704 | tf_op jit(solution)/shard_map/sk,kwr->swr/dot_general | solution.py:18
  28.9 0.0 copy-start.8
  28.9 2.5 copy.51
  31.4 0.0 reduce-scatter.2.cloned.1.call-update
  31.4 0.0 copy-start.4
  31.5 0.0 all-reduce.3.cloned.1.call-start
  31.5 0.0 copy-done.8
  31.5 0.6 dynamic_slice.3
  32.1 0.6 compare_convert_fusion
  32.8 69.3 %reduce-scatter.2.cloned.1.call-done = f32[1,128,512]{2,1,0:T(8,128)} async-done(((f32[8,128,512]{2,1,0:T(8,128)}), f32[1,128,512]{2,1,0:T(8,128)}) %reduce-scatter.2.cloned.1.call-update) | async-done | bytes 262160 | tf_op jit(solution)/shard_map/reduce_scatter | solution.py:45
  102.1 1.2 convolution_convert_fusion.6
  103.3 1.6 convolution_bitcast_fusion.2
  105.0 1.8 copy.52
  106.7 2.6 broadcast_multiply_fusion
  109.3 0.0 all-reduce.3.cloned.1.call-update
  109.4 0.0 all-reduce.5.cloned.1.call-start
  109.4 101.0 %all-reduce.3.cloned.1.call-done = f32[8,128,512]{2,1,0:T(8,128)} async-done(((f32[8,128,512]{2,1,0:T(8,128)}), f32[8,128,512]{2,1,0:T(8,128)}) %all-reduce.3.cloned.1.call-update) | async-done | bytes 2097168 | tf_op jit(solution)/shard_map/psum | solution.py:55
  210.4 0.0 copy-done.4
  210.4 0.0 copy-start.5
  210.4 2.4 convolution_convert_fusion.2
  212.8 0.0 copy-start.2
  212.8 1.0 copy-done.2
  213.8 0.0 copy-done.5
  213.8 0.0 copy-start.6
  213.8 1.8 convolution_bitcast_fusion.1
  215.5 3.1 copy.54
  218.6 0.0 copy-done.6
  218.6 2.7 fusion.26
  221.3 1.3 copy.55
  222.6 0.0 all-reduce.5.cloned.1.call-update
  222.6 0.2 all-gather.3.cloned.1.call-start
  224.8 33.8 %all-reduce.5.cloned.1.call-done = f32[4,128,512]{2,1,0:T(8,128)} async-done(((f32[4,128,512]{2,1,0:T(8,128)}), f32[4,128,512]{2,1,0:T(8,128)}) %all-reduce.5.cloned.1.call-update) | async-done | bytes 1048592 | tf_op jit(solution)/shard_map/psum | solution.py:59
  258.6 2.7 fusion.7
  261.3 2.7 gather_fusion
  264.0 3.3 convolution_convert_fusion.1
  267.4 1.9 convolution_convert_fusion.5
  269.2 0.0 all-gather.3.cloned.1.call-update
  269.3 2.0 copy.64
  271.3 1.7 copy.62
  273.0 2.3 copy.63
  275.2 34.1 %all-gather.3.cloned.1.call-done = bf16[1024,512]{0,1:T(8,128)(2,1)} async-done(((bf16[128,512]{0,1:T(8,128)(2,1)}), bf16[1024,512]{0,1:T(8,128)(2,1)}) %all-gather.3.cloned.1.call-update) | async-done | bytes 1048592 | tf_op jit(solution)/shard_map/all_gather | solution.py:71
  309.3 2.3 copy.71
  311.6 3.7 %gather_fusion.1 = bf16[24,128,512]{2,1,0:T(8,128)(2,1)} fusion(bf16[8,128,512]{2,1,0:T(8,128)(2,1)} %bitcast.68, s32[1024]{0:T(1024)S(1)} %pad_clamp_fusion), kind=kCustom, calls=%fused_computation.1 | custom fusion | bytes 6291552 | tf_op jit(solution)/shard_map/gather | solution.py:73
  315.3 6.8 %convert_bitcast_fusion = bf16[24,128,512]{1,2,0:T(8,128)(2,1)} fusion(bf16[24,128,128]{2,1,0:T(8,128)(2,1)} %param.15, bf16[24,128,512]{2,1,0:T(8,128)(2,1)} %copy-done.1, bf16[24,128,512]{2,1,0:T(8,128)(2,1)} %gather_fusion.1, bf16[24,128,128]{2,1,0:T(8,128)(2,1)} %param.16), kind=kOutput, calls=%fused_computation.5 | convolution fusion | flops 811597824 | bytes 11010048 | tf_op jit(solution)/shard_map/nij,nir->njr/dot_general | solution.py:12
  322.1 4.6 %copy.61 = bf16[24,128,512]{2,1,0:T(8,128)(2,1)} copy(bf16[24,128,512]{1,2,0:T(8,128)(2,1)} %convert_bitcast_fusion) | data formatting | bytes 6291456
  (5 shorter events, 0.0 us)
Async XLA Ops:
  7.2 1.9 copy-start
  7.2 94.9 %reduce-scatter.2.cloned.1.call-start = ((), (), s32[]{:S(2)}) async-start(), calls=%async_computation.1 | async-start | bytes 2359296 | tf_op jit(solution)/shard_map/reduce_scatter | solution.py:45
  9.1 3.8 %copy-start.3 = (bf16[24,128,128]{2,1,0:T(8,128)(2,1)S(1)}, bf16[24,128,128]{2,1,0:T(8,128)(2,1)}, u32[]{:S(2)}) copy-start(bf16[24,128,128]{2,1,0:T(8,128)(2,1)} %param.16) | copy-start | bytes 2359300
  11.2 1.7 copy-start.1
  16.6 6.7 %copy-start.7 = (s32[24]{0:T(128)S(1)}, s32[24]{0:T(128)}, u32[]{:S(2)}) copy-start(s32[24]{0:T(128)} %param.17) | copy-start | bytes 292
  28.9 2.6 copy-start.8
  31.4 178.9 %copy-start.4 = (bf16[8,128,128]{2,1,0:T(8,128)(2,1)S(1)}, bf16[8,128,128]{2,1,0:T(8,128)(2,1)}, u32[]{:S(2)}) copy-start(bf16[8,128,128]{2,1,0:T(8,128)(2,1)} %param.23) | copy-start | bytes 786436
  31.5 178.9 %all-reduce.3.cloned.1.call-start = ((), (), s32[]{:S(2)}) async-start(), calls=%async_computation.2 | async-start | bytes 4194304 | tf_op jit(solution)/shard_map/psum | solution.py:55
  109.4 149.3 %all-reduce.5.cloned.1.call-start = ((), (), s32[]{:S(2)}) async-start(), calls=%async_computation.3 | async-start | bytes 2097152 | tf_op jit(solution)/shard_map/psum | solution.py:59
  210.4 3.4 %copy-start.5 = (bf16[8,128,128]{2,1,0:T(8,128)(2,1)S(1)}, bf16[8,128,128]{2,1,0:T(8,128)(2,1)}, u32[]{:S(2)}) copy-start(bf16[8,128,128]{2,1,0:T(8,128)(2,1)} %param.24) | copy-start | bytes 786436
  212.8 1.0 copy-start.2
  213.8 4.8 %copy-start.6 = (s32[8]{0:T(128)S(1)}, s32[8]{0:T(128)}, u32[]{:S(2)}) copy-start(s32[8]{0:T(128)} %param.25) | copy-start | bytes 100
  222.6 86.7 %all-gather.3.cloned.1.call-start = ((), (), s32[]{:S(2)}) async-start(), calls=%async_computation.4 | async-start | bytes 1179648 | tf_op jit(solution)/shard_map/all_gather | solution.py:71
Sparse Core Ops, SparseCore 0:
  31.6 70.4 reduce-scatter.1
  109.5 100.8 all-reduce.2
  222.8 35.8 all-reduce.4
  269.4 39.9 all-gather.2
where the time goes:
time: 334 us; the launch traced here: 333 us
  waiting for transfers between devices  238 us (71%)
  local copies, waits for them, and re-layouts  39.8 us (12%)
  matrix products  35.8 us (11%)
  between operations  15.8 us (5%)
    psum x1, waiting for transfers between devices, local(): middle_sum = lax.psum(middle_term, 'col')  101 us
    reduce_scatter x1, waiting for transfers between devices, local(): lax.psum_scatter(slot_sums(leaf_target, lax.axis_size('col') * 1, leaf_up...  69.3 us
    all_gather x1, waiting for transfers between devices, local(): row_result = lax.all_gather(node_result, 'col', axis=0, tiled=True)  34.1 us
    psum x1, waiting for transfers between devices, local(): top_sum = lax.psum(top_term, 'row')  33.8 us
    unnamed x22, local copies, waits for them, and re-layouts  15.1 us
    dot_general x4, matrix products, apply_transposed(): jnp.einsum('nij,nir->njr', matrix, vectors, preferred_element_type=jnp.fl...  14.7 us
    dot_general x6, matrix products, apply_block(): jnp.einsum('nij,njr->nir', matrix, vectors, preferred_element_type=jnp.fl...  12.9 us
    dot_general x3, local copies, waits for them, and re-layouts, apply_block(): jnp.einsum('nij,njr->nir', matrix, vectors, preferred_element_type=jnp.fl...  11.6 us
  transfers between devices with their start and end apart: 4, of which 4 were waited for; matrix products, arithmetic and copies ran while one was open for 2% of the time, Pallas kernels for 0%

commit v1 on v0

v1 whole, which is shorter than its diff:
```python
import functools

import jax
import jax.numpy as jnp
from jax import lax
from jax.experimental import pallas as pl
from jax.experimental.pallas import tpu as pltpu
from jax.sharding import PartitionSpec as P

MESH = pl.DeviceIdType.MESH
F32 = jnp.float32
BF16 = jnp.bfloat16
VMEM_LIMIT = 56 * 1024 * 1024


def mul(a, b):
    return jnp.dot(a, b, preferred_element_type=F32)


def mul_t(a, b):
    return lax.dot_general(a, b, (((0,), (0,)), ((), ())), preferred_element_type=F32)


def leaf_forward_kernel(steps, block, peers, target, rhs, inverse, link, solved, sums, total):
    step = pl.program_id(0)

    @pl.when(step == 0)
    def _():
        total[...] = jnp.zeros_like(total)

    for i in range(block):
        part = mul(inverse[i], rhs[i]).astype(BF16)
        solved[i] = part
        slot = target[step * block + i] % peers
        total[slot] += mul(link[i], part)

    @pl.when(step == steps - 1)
    def _():
        sums[...] = total[...].astype(BF16)


def leaf_backward_kernel(block, peers, target, solved, inverse, link, above, result):
    step = pl.program_id(0)
    for i in range(block):
        slot = target[step * block + i] % peers
        w = (solved[i].astype(F32) - mul_t(link[i], above[slot])).astype(BF16)
        result[i] = mul_t(inverse[i], w).astype(BF16)


def bits_of(index, count):
    return [(index // (1 << b)) % 2 for b in range(count)]


def log2(n):
    return n.bit_length() - 1


def tree_kernel(
    rows,
    peers,
    part,
    node_rhs,
    node_inverse,
    node_link,
    node_parent,
    middle_rhs,
    middle_inverse,
    middle_link,
    middle_parent,
    top_rhs,
    top_inverse,
    row_out,
    middle_out,
    top_out,
    work,
    landed,
    updates,
    choose,
    middle_solved,
    top_choose,
    top_term,
    top_landed,
    top_step,
    top_half,
    rs_send,
    rs_recv,
    up_send,
    up_recv,
    down_send,
    down_recv,
    row_send,
    row_recv,
):
    row, me = lax.axis_index("row"), lax.axis_index("col")
    width, columns = node_rhs.shape[1:]
    half = columns // 2
    halves = [slice(0, half), slice(half, columns)]
    middles, tops = middle_rhs.shape[0], top_rhs.shape[0]
    levels, row_levels = log2(peers), log2(rows)
    mine, row_mine = bits_of(me, levels), bits_of(row, row_levels)
    partner = [me + (1 - 2 * mine[b]) * (1 << b) for b in range(levels)]
    row_partner = [row + (1 - 2 * row_mine[b]) * (1 << b) for b in range(row_levels)]

    barrier = pltpu.get_barrier_semaphore()
    for p in partner:
        pl.semaphore_signal(barrier, inc=1, device_id=(row, p), device_id_type=MESH)
    for p in row_partner:
        pl.semaphore_signal(barrier, inc=1, device_id=(p, me), device_id_type=MESH)
    pl.semaphore_wait(barrier, levels + row_levels)

    first = list(range(levels))
    second = [1, 0] + first[2:] if levels > 1 else first
    orders = [first, second]
    pending = []

    def slot_of(flip):
        slot = 0
        for b in range(levels):
            bit = 1 - mine[b] if flip.get(b) else mine[b]
            slot = slot + bit * (1 << b)
        return slot

    def scatter_slot(h, k, j, sent):
        order = orders[h]
        free = order[k + 1 :]
        flip = {b: (j >> (len(free) - 1 - i)) & 1 for i, b in enumerate(free)}
        flip[order[k]] = sent
        return slot_of(flip)

    def scatter_place(k, j):
        return sum(1 << (levels - 1 - i) for i in range(k)) + j

    scatter = {}

    def scatter_start(h, k, j):
        slot = scatter_slot(h, k, j, 1)
        place = scatter_place(k, j)
        source = part if k == 0 else work
        copy = pltpu.make_async_remote_copy(
            src_ref=source.at[slot, :, halves[h]],
            dst_ref=landed.at[h, place],
            send_sem=rs_send.at[h, place],
            recv_sem=rs_recv.at[h, place],
            device_id=(row, partner[orders[h][k]]),
            device_id_type=MESH,
        )
        copy.start()
        scatter[h, k, j] = copy
        pending.append(copy)

    def scatter_add(h, k, j):
        scatter[h, k, j].wait_recv()
        slot = scatter_slot(h, k, j, 0)
        source = part if k == 0 else work
        return slot, source[slot, :, halves[h]].astype(F32) + landed[h, scatter_place(k, j)].astype(F32)

    for j in reversed(range(1 << (levels - 1))):
        for h in range(2):
            scatter_start(h, 0, j)

    eye = (
        lax.broadcasted_iota(jnp.int32, (width, width), 0) == lax.broadcasted_iota(jnp.int32, (width, width), 1)
    ).astype(F32)
    for c in range(peers):
        slot = node_parent[c] % middles
        for p in range(middles):
            choose[p, :, c * width : (c + 1) * width] = (eye * jnp.where(slot == p, 1.0, 0.0)).astype(BF16)
    for k in range(middles):
        slot = middle_parent[k]
        block = middle_link[k].astype(F32)
        for p in range(tops):
            top_choose[p, :, k * width : (k + 1) * width] = jnp.where(slot == p, block, 0.0).astype(BF16)

    for k in range(1, levels):
        count = 1 << (levels - 1 - k)
        for j in reversed(range(2 * count)):
            for h in range(2):
                slot, value = scatter_add(h, k - 1, j)
                work[slot, :, halves[h]] = value.astype(BF16)
                if j >= count:
                    scatter_start(h, k, j - count)

    def gather_slot(h, done, j):
        flip = {b: (j >> i) & 1 for i, b in enumerate(done)}
        return slot_of(flip)

    def gather_copy(buffer, send, recv, h, k, j):
        order = orders[h][::-1]
        slot = gather_slot(h, order[:k], j)
        place = (1 << k) - 1 + j
        view = buffer.at[slot, :, halves[h]]
        return pltpu.make_async_remote_copy(
            src_ref=view,
            dst_ref=view,
            send_sem=send.at[h, place],
            recv_sem=recv.at[h, place],
            device_id=(row, partner[order[k]]),
            device_id_type=MESH,
        )

    def gather_rest(buffer, send, recv, copies):
        for k in range(1, levels):
            for j in range(1 << k):
                for h in range(2):
                    old = 1 << (k - 1)
                    if j >= old:
                        copies[h, k - 1, j - old].wait_recv()
                    copy = gather_copy(buffer, send, recv, h, k, j)
                    copy.start()
                    copies[h, k, j] = copy
        for j in range(1 << (levels - 1)):
            for h in range(2):
                copies[h, levels - 1, j].wait_recv()
        pending.extend(copies.values())

    copies = {}
    node_solved = []
    for h in range(2):
        _, total = scatter_add(h, levels - 1, 0)
        node_y = (node_rhs[0, :, halves[h]].astype(F32) - total).astype(BF16)
        solved = mul(node_inverse[0], node_y).astype(BF16)
        updates[me, :, halves[h]] = mul(node_link[0], solved).astype(BF16)
        copies[h, 0, 0] = gather_copy(updates, up_send, up_recv, h, 0, 0)
        copies[h, 0, 0].start()
        node_solved.append(solved)
    gather_rest(updates, up_send, up_recv, copies)

    def middle_forward(p, carry):
        total = mul(choose[p], updates[...].reshape(peers * width, columns))
        middle_y = (middle_rhs[p].astype(F32) - total).astype(BF16)
        middle_solved[p] = mul(middle_inverse[p], middle_y).astype(BF16)
        return carry

    lax.fori_loop(0, middles, middle_forward, 0)

    for p in range(tops):
        total = mul(top_choose[p], middle_solved[...].reshape(middles * width, columns)).astype(BF16)
        for h in range(2):
            top_term[h, p] = total[:, halves[h]]

    core = row_mine[0]
    for k in range(row_levels):
        copy = pltpu.make_async_remote_copy(
            src_ref=top_term.at[1 - core] if k == 0 else top_step.at[k - 1],
            dst_ref=top_landed.at[k],
            send_sem=row_send.at[k],
            recv_sem=row_recv.at[k],
            device_id=(row_partner[k], me),
            device_id_type=MESH,
        )
        copy.start()
        pending.append(copy)
        copy.wait_recv()
        if k < row_levels - 1:
            held = top_term[core] if k == 0 else top_step[k - 1]
            top_step[k] = (held.astype(F32) + top_landed[k].astype(F32)).astype(BF16)
    for p in range(tops):
        last = row_levels - 1
        held = top_term[core, p] if last == 0 else top_step[last - 1, p]
        total = held.astype(F32) + top_landed[last, p].astype(F32)
        rhs = top_rhs[p].astype(F32)
        rhs = jnp.where(core == 0, rhs[:, :half], rhs[:, half:])
        solved = mul(top_inverse[p], (rhs - total).astype(BF16)).astype(BF16)
        top_half[core, p] = mul_t(top_inverse[p], solved).astype(BF16)
    view = top_half.at[core]
    copy = pltpu.make_async_remote_copy(
        src_ref=view,
        dst_ref=view,
        send_sem=row_send.at[row_levels],
        recv_sem=row_recv.at[row_levels],
        device_id=(row_partner[0], me),
        device_id_type=MESH,
    )
    copy.start()
    pending.append(copy)
    copy.wait_recv()
    for p in range(tops):
        for h in range(2):
            top_out[p, :, halves[h]] = top_half[h, p]

    def middle_backward(k):
        above = top_out[middle_parent[k]]
        w = (middle_solved[k].astype(F32) - mul_t(middle_link[k], above)).astype(BF16)
        return mul_t(middle_inverse[k], w).astype(BF16)

    own = middle_backward(node_parent[me] % middles)
    copies = {}
    for h in range(2):
        node_w = (node_solved[h].astype(F32) - mul_t(node_link[0], own[:, halves[h]])).astype(BF16)
        row_out[me, :, halves[h]] = mul_t(node_inverse[0], node_w).astype(BF16)
        copies[h, 0, 0] = gather_copy(row_out, down_send, down_recv, h, 0, 0)
        copies[h, 0, 0].start()

    def middle_store(k, carry):
        middle_out[k] = middle_backward(k)
        return carry

    lax.fori_loop(0, middles, middle_store, 0)
    gather_rest(row_out, down_send, down_recv, copies)
    for copy in pending:
        copy.wait_send()


def local(
    rows,
    peers,
    leaf_rhs,
    leaf_inverse,
    leaf_link,
    leaf_parent,
    node_rhs,
    node_inverse,
    node_link,
    node_parent,
    middle_rhs,
    middle_inverse,
    middle_link,
    middle_parent,
    top_rhs,
    top_inverse,
):
    leaves, width, columns = leaf_rhs.shape
    middles, tops = middle_rhs.shape[0], top_rhs.shape[0]
    half = columns // 2
    levels, row_levels = log2(peers), log2(rows)
    block = max(b for b in (1, 2, 3, 4) if leaves % b == 0)
    steps = leaves // block
    vectors = pl.BlockSpec((block, width, columns), lambda i, t: (i, 0, 0))
    matrices = pl.BlockSpec((block, width, width), lambda i, t: (i, 0, 0))
    slots = pl.BlockSpec((peers, width, columns), lambda i, t: (0, 0, 0))
    leaf_solved, sums = pl.pallas_call(
        functools.partial(leaf_forward_kernel, steps, block, peers),
        grid_spec=pltpu.PrefetchScalarGridSpec(
            num_scalar_prefetch=1,
            grid=(steps,),
            in_specs=[vectors, matrices, matrices],
            out_specs=[vectors, slots],
            scratch_shapes=[pltpu.VMEM((peers, width, columns), F32)],
        ),
        out_shape=[
            jax.ShapeDtypeStruct(leaf_rhs.shape, BF16),
            jax.ShapeDtypeStruct((peers, width, columns), BF16),
        ],
        compiler_params=pltpu.CompilerParams(vmem_limit_bytes=VMEM_LIMIT),
        name="leaf_forward",
    )(leaf_parent, leaf_rhs, leaf_inverse, leaf_link)

    vmem = pl.BlockSpec(memory_space=pltpu.VMEM)
    smem = pl.BlockSpec(memory_space=pltpu.SMEM)
    dma = pltpu.SemaphoreType.DMA
    row_result, middle_result, top_result = pl.pallas_call(
        functools.partial(tree_kernel, rows, peers),
        in_specs=[vmem] * 4 + [smem] + [vmem] * 3 + [smem] + [vmem] * 2,
        out_specs=[vmem] * 3,
        out_shape=[
            jax.ShapeDtypeStruct((peers, width, columns), BF16),
            jax.ShapeDtypeStruct(middle_rhs.shape, BF16),
            jax.ShapeDtypeStruct(top_rhs.shape, BF16),
        ],
        scratch_shapes=[
            pltpu.VMEM((peers, width, columns), BF16),
            pltpu.VMEM((2, peers - 1, width, half), BF16),
            pltpu.VMEM((peers, width, columns), BF16),
            pltpu.VMEM((middles, width, peers * width), BF16),
            pltpu.VMEM((middles, width, columns), BF16),
            pltpu.VMEM((tops, width, middles * width), BF16),
            pltpu.VMEM((2, tops, width, half), BF16),
            pltpu.VMEM((row_levels, tops, width, half), BF16),
            pltpu.VMEM((row_levels, tops, width, half), BF16),
            pltpu.VMEM((2, tops, width, half), BF16),
            dma((2, peers - 1)),
            dma((2, peers - 1)),
            dma((2, peers - 1)),
            dma((2, peers - 1)),
            dma((2, peers - 1)),
            dma((2, peers - 1)),
            dma((row_levels + 1,)),
            dma((row_levels + 1,)),
        ],
        compiler_params=pltpu.CompilerParams(
            collective_id=0, has_side_effects=True, vmem_limit_bytes=VMEM_LIMIT
        ),
        name="tree",
    )(
        sums,
        node_rhs,
        node_inverse,
        node_link,
        node_parent,
        middle_rhs,
        middle_inverse,
        middle_link,
        middle_parent,
        top_rhs,
        top_inverse,
    )
    node_result = lax.dynamic_slice_in_dim(row_result, lax.axis_index("col"), 1)

    leaf_result = pl.pallas_call(
        functools.partial(leaf_backward_kernel, block, peers),
        grid_spec=pltpu.PrefetchScalarGridSpec(
            num_scalar_prefetch=1,
            grid=(steps,),
            in_specs=[vectors, matrices, matrices, slots],
            out_specs=vectors,
        ),
        out_shape=jax.ShapeDtypeStruct(leaf_rhs.shape, BF16),
        compiler_params=pltpu.CompilerParams(vmem_limit_bytes=VMEM_LIMIT),
        name="leaf_backward",
    )(leaf_parent, leaf_solved, leaf_inverse, leaf_link, row_result)
    return (leaf_result, node_result, middle_result, top_result)


def solution(mesh):
    placed = (
        P(("row", "col"), None, None),
        P(("row", "col"), None, None),
        P(("row", "col"), None, None),
        P(("row", "col")),
        P(("row", "col"), None, None),
        P(("row", "col"), None, None),
        P(("row", "col"), None, None),
        P("row"),
        P("row", None, None),
        P("row", None, None),
        P("row", None, None),
        P("row"),
        P(),
        P(),
    )
    return jax.shard_map(
        functools.partial(local, mesh.shape["row"], mesh.shape["col"]),
        mesh=mesh,
        in_specs=placed,
        out_specs=(
            P(("row", "col"), None, None),
            P(("row", "col"), None, None),
            P("row", None, None),
            P(),
        ),
        check_vma=False,
    )
```

time: 334 us -> 92.3 us (0.28)
  waiting for transfers between devices: 238 us -> 0 us
  Pallas kernels: 0 us -> 87.8 us
  local copies, waits for them, and re-layouts: 39.8 us -> 3.34 us
  matrix products: 35.8 us -> 0 us
  between operations: 15.8 us -> 0.66 us
    psum x2 -> x0, waiting for transfers between devices: 135 us -> none  [the longest x1 101 us: local(): middle_sum = lax.psum(middle_term, 'col')]
    pallas_call x0 -> x3, Pallas kernels: none -> 87.8 us  [the longest x1 68.4 us: local(): pl.pallas_call(functools.partial(tree_kernel, rows, peers), in_specs=[vme...]
    reduce_scatter x1 -> x0, waiting for transfers between devices: 69.3 us -> none  [local(): lax.psum_scatter(slot_sums(leaf_target, lax.axis_size('col') * 1, leaf_up...]
    dot_general x12 -> x0, matrix products: 35.8 us -> none  [the longest x4 14.7 us: apply_transposed(): jnp.einsum('nij,nir->njr', matrix, vectors, preferred_element_type=jnp.fl...]
    all_gather x1 -> x0, waiting for transfers between devices: 34.1 us -> none  [local(): row_result = lax.all_gather(node_result, 'col', axis=0, tiled=True)]
    dot_general x5 -> x0, local copies, waits for them, and re-layouts: 15.4 us -> none  [the longest x3 11.6 us: apply_block(): jnp.einsum('nij,njr->nir', matrix, vectors, preferred_element_type=jnp.fl...]
    unnamed x22 -> x6, local copies, waits for them, and re-layouts: 15.1 us -> 1.77 us
    gather x2 -> x0, local copies, waits for them, and re-layouts: 6.4 us -> none  [the longest x1 3.71 us: local(): row_result[leaf_target]]
  transfers between devices with their start and end apart: 4 -> 0, of which waited for: 4 -> 0; matrix products, arithmetic and copies ran while one was open for 2% -> 0% of each run, Pallas kernels for 0% -> 0%
where the time goes in v1:
time: 92.3 us; the launch traced here: 91.8 us
  Pallas kernels  87.8 us (95%)
  local copies, waits for them, and re-layouts  3.34 us (4%)
    pallas_call x1, Pallas kernels, local(): pl.pallas_call(functools.partial(tree_kernel, rows, peers), in_specs=[vme...  68.4 us
    pallas_call x1, Pallas kernels, local(): pl.pallas_call(functools.partial(leaf_backward_kernel, block, peers), gri...  9.72 us
    pallas_call x1, Pallas kernels, local(): pl.pallas_call(functools.partial(leaf_forward_kernel, steps, block, peers...  9.66 us

profile of v1, /device:TPU:0, one launch (start us, length us, event | category | flops | bytes accessed | tf_op | source)
XLA Modules:
  0.0 91.8 jit_solution(6144704786926839071)
XLA Ops:
  0.6 9.7 %leaf_forward.1 = (bf16[24,128,512]{2,1,0:T(8,128)(2,1)}, bf16[8,128,512]{2,1,0:T(8,128)(2,1)}) custom-call(s32[24]{0:T(128)} %target.3, bf16[24,128,512]{2,1,0:T(8,128)(2,1)} %rhs.1, bf16[24,128,128]{2,1,0:T(8,128)(2,1)} %inverse.3, bf16[24,128,128]{2,1,0:T(8,128)(2,1)} %link.3), custom_call_target="tpu_custom_call" | custom-call | tf_op jit(solution)/shard_map/leaf_forward/pallas_call | solution.py:331
  10.3 68.4 %tree.1 = (bf16[8,128,512]{2,1,0:T(8,128)(2,1)}, bf16[8,128,512]{2,1,0:T(8,128)(2,1)}, bf16[4,128,512]{2,1,0:T(8,128)(2,1)}) custom-call(bf16[8,128,512]{2,1,0:T(8,128)(2,1)} %get-tuple-element.10.part, bf16[1,128,512]{2,1,0:T(8,128)(2,1)} %node_rhs.1, bf16[1,128,128]{2,1,0:T(8,128)(2,1)} %node_inverse.1, bf16[1,128,128]{2,1,0:T(8,128)(2,1)} %node_link.1, ...), custom_call_target="tpu_custom_call" | custom-call | tf_op jit(solution)/shard_map/tree/pallas_call | solution.py:351
  78.8 0.0 copy-start
  78.8 0.0 copy-start.1
  78.8 9.7 %leaf_backward.1 = bf16[24,128,512]{2,1,0:T(8,128)(2,1)} custom-call(s32[24]{0:T(128)} %target.3, bf16[24,128,512]{2,1,0:T(8,128)(2,1)} %get-tuple-element.9.solved, bf16[24,128,128]{2,1,0:T(8,128)(2,1)} %inverse.3, bf16[24,128,128]{2,1,0:T(8,128)(2,1)} %link.3, bf16[8,128,512]{2,1,0:T(8,128)(2,1)} %get-tuple-element.11.above), custom_call_target="tpu_custom_call" | custom-call | tf_op jit(solution)/shard_map/leaf_backward/pallas_call | solution.py:399
  88.5 1.6 %constant_dynamic-slice_fusion = bf16[1,128,512]{2,1,0:T(8,128)(2,1)} fusion(bf16[8,128,512]{2,1,0:T(8,128)(2,1)} %get-tuple-element.11.above, s32[]{:T(128)S(6)} %select_n.3), kind=kLoop, calls=%fused_computation | loop fusion | bytes 262148 | tf_op jit(solution)/shard_map/dynamic_slice | solution.py:397
  90.1 0.0 copy-done
  90.1 1.0 %copy.20 = bf16[8,128,512]{2,1,0:T(8,128)(2,1)} copy(bf16[8,128,512]{2,1,0:T(8,128)(2,1)S(1)} %copy-done) | data formatting | bytes 2097152
  91.0 0.0 copy-done.1
  91.0 0.8 copy.21
Async XLA Ops:
  78.8 11.3 %copy-start = (bf16[8,128,512]{2,1,0:T(8,128)(2,1)S(1)}, bf16[8,128,512]{2,1,0:T(8,128)(2,1)}, u32[]{:S(2)}) copy-start(bf16[8,128,512]{2,1,0:T(8,128)(2,1)} %get-tuple-element.20) | copy-start | bytes 3145732
  78.8 12.3 %copy-start.1 = (bf16[4,128,512]{2,1,0:T(8,128)(2,1)S(1)}, bf16[4,128,512]{2,1,0:T(8,128)(2,1)}, u32[]{:S(2)}) copy-start(bf16[4,128,512]{2,1,0:T(8,128)(2,1)} %get-tuple-element.21) | copy-start | bytes 1572868

commit v2 on v1

--- a/solution.py
+++ b/solution.py
@@ -28,23 +28,41 @@
     def _():
         total[...] = jnp.zeros_like(total)
 
+    parts = [mul(inverse[i], rhs[i]).astype(BF16) for i in range(block)]
     for i in range(block):
-        part = mul(inverse[i], rhs[i]).astype(BF16)
-        solved[i] = part
+        solved[i] = parts[i]
+    updates = [mul(link[i], parts[i]) for i in range(block)]
+    for i in range(block):
         slot = target[step * block + i] % peers
-        total[slot] += mul(link[i], part)
+        total[slot] += updates[i]
 
     @pl.when(step == steps - 1)
     def _():
         sums[...] = total[...].astype(BF16)
 
 
-def leaf_backward_kernel(block, peers, target, solved, inverse, link, above, result):
+def leaf_backward_kernel(
+    steps, block, peers, target, solved, inverse, link, above, node, middle, top, result, node_out, middle_out, top_out, sem
+):
     step = pl.program_id(0)
+    pairs = [(node, node_out), (middle, middle_out), (top, top_out)]
+    passed = [pltpu.make_async_copy(src, dst, sem.at[i]) for i, (src, dst) in enumerate(pairs)]
+
+    @pl.when(step == 0)
+    def _():
+        for copy in passed:
+            copy.start()
+
+    parents = [above[target[step * block + i] % peers] for i in range(block)]
+    w = [(solved[i].astype(F32) - mul_t(link[i], parents[i])).astype(BF16) for i in range(block)]
+    results = [mul_t(inverse[i], w[i]).astype(BF16) for i in range(block)]
     for i in range(block):
-        slot = target[step * block + i] % peers
-        w = (solved[i].astype(F32) - mul_t(link[i], above[slot])).astype(BF16)
-        result[i] = mul_t(inverse[i], w).astype(BF16)
+        result[i] = results[i]
+
+    @pl.when(step == steps - 1)
+    def _():
+        for copy in passed:
+            copy.wait()
 
 
 def bits_of(index, count):
@@ -63,15 +81,24 @@
     node_inverse,
     node_link,
     node_parent,
+    middle_rhs_hbm,
+    middle_inverse_hbm,
+    middle_link_hbm,
+    middle_parent,
+    top_rhs_hbm,
+    top_inverse_hbm,
+    row_out,
+    node_out,
+    middle_hbm,
+    top_hbm,
     middle_rhs,
     middle_inverse,
     middle_link,
-    middle_parent,
     top_rhs,
     top_inverse,
-    row_out,
     middle_out,
     top_out,
+    local_sem,
     work,
     landed,
     updates,
@@ -158,18 +185,27 @@
         for h in range(2):
             scatter_start(h, 0, j)
 
+    sources = [middle_link_hbm, middle_inverse_hbm, middle_rhs_hbm, top_rhs_hbm, top_inverse_hbm]
+    places = [middle_link, middle_inverse, middle_rhs, top_rhs, top_inverse]
+    fetched = [pltpu.make_async_copy(sources[i], places[i], local_sem.at[i]) for i in range(5)]
+    for copy in fetched:
+        copy.start()
+
     eye = (
         lax.broadcasted_iota(jnp.int32, (width, width), 0) == lax.broadcasted_iota(jnp.int32, (width, width), 1)
     ).astype(F32)
     for c in range(peers):
         slot = node_parent[c] % middles
         for p in range(middles):
-            choose[p, :, c * width : (c + 1) * width] = (eye * jnp.where(slot == p, 1.0, 0.0)).astype(BF16)
+            choose[p * width : (p + 1) * width, c * width : (c + 1) * width] = (eye * jnp.where(slot == p, 1.0, 0.0)).astype(BF16)
+    fetched[0].wait()
     for k in range(middles):
         slot = middle_parent[k]
         block = middle_link[k].astype(F32)
         for p in range(tops):
-            top_choose[p, :, k * width : (k + 1) * width] = jnp.where(slot == p, block, 0.0).astype(BF16)
+            top_choose[p * width : (p + 1) * width, k * width : (k + 1) * width] = jnp.where(slot == p, block, 0.0).astype(BF16)
+    for copy in fetched[1:]:
+        copy.wait()
 
     for k in range(1, levels):
         count = 1 << (levels - 1 - k)
@@ -198,20 +234,17 @@
             device_id_type=MESH,
         )
 
-    def gather_rest(buffer, send, recv, copies):
-        for k in range(1, levels):
-            for j in range(1 << k):
-                for h in range(2):
-                    old = 1 << (k - 1)
-                    if j >= old:
-                        copies[h, k - 1, j - old].wait_recv()
-                    copy = gather_copy(buffer, send, recv, h, k, j)
-                    copy.start()
-                    copies[h, k, j] = copy
-        for j in range(1 << (levels - 1)):
+    def gather_forward(buffer, send, recv, copies, h, k, j):
+        for later in range(k, levels):
+            copy = gather_copy(buffer, send, recv, h, later, j)
+            copy.start()
+            copies[h, later, j] = copy
+
+    def gather_level(buffer, send, recv, copies, k):
+        for j in range(1 << k):
             for h in range(2):
-                copies[h, levels - 1, j].wait_recv()
-        pending.extend(copies.values())
+                copies[h, k, j].wait_recv()
+                gather_forward(buffer, send, recv, copies, h, k + 1, j + (1 << k))
 
     copies = {}
     node_solved = []
@@ -220,63 +253,71 @@
         node_y = (node_rhs[0, :, halves[h]].astype(F32) - total).astype(BF16)
         solved = mul(node_inverse[0], node_y).astype(BF16)
         updates[me, :, halves[h]] = mul(node_link[0], solved).astype(BF16)
-        copies[h, 0, 0] = gather_copy(updates, up_send, up_recv, h, 0, 0)
-        copies[h, 0, 0].start()
+        gather_forward(updates, up_send, up_recv, copies, h, 0, 0)
         node_solved.append(solved)
-    gather_rest(updates, up_send, up_recv, copies)
-
-    def middle_forward(p, carry):
-        total = mul(choose[p], updates[...].reshape(peers * width, columns))
-        middle_y = (middle_rhs[p].astype(F32) - total).astype(BF16)
-        middle_solved[p] = mul(middle_inverse[p], middle_y).astype(BF16)
-        return carry
-
-    lax.fori_loop(0, middles, middle_forward, 0)
-
-    for p in range(tops):
-        total = mul(top_choose[p], middle_solved[...].reshape(middles * width, columns)).astype(BF16)
-        for h in range(2):
-            top_term[h, p] = total[:, halves[h]]
+    for k in range(levels):
+        gather_level(updates, up_send, up_recv, copies, k)
+    pending.extend(copies.values())
+
+    gathered = updates[...].reshape(peers * width, columns)
+    group = max(g for g in (1, 2, 4) if middles % g == 0)
+    for start in range(0, middles, group):
+        total = mul(choose[start * width : (start + group) * width], gathered)
+        for i in range(group):
+            p = start + i
+            middle_y = (middle_rhs[p].astype(F32) - total[i * width : (i + 1) * width]).astype(BF16)
+            middle_solved[p] = mul(middle_inverse[p], middle_y).astype(BF16)
 
     core = row_mine[0]
-    for k in range(row_levels):
+    last = row_levels - 1
+
+    def row_start(source, target, k, p, to):
         copy = pltpu.make_async_remote_copy(
-            src_ref=top_term.at[1 - core] if k == 0 else top_step.at[k - 1],
-            dst_ref=top_landed.at[k],
-            send_sem=row_send.at[k],
-            recv_sem=row_recv.at[k],
-            device_id=(row_partner[k], me),
+            src_ref=source,
+            dst_ref=target,
+            send_sem=row_send.at[k, p],
+            recv_sem=row_recv.at[k, p],
+            device_id=(row_partner[to], me),
             device_id_type=MESH,
         )
         copy.start()
         pending.append(copy)
-        copy.wait_recv()
-        if k < row_levels - 1:
-            held = top_term[core] if k == 0 else top_step[k - 1]
-            top_step[k] = (held.astype(F32) + top_landed[k].astype(F32)).astype(BF16)
+        return copy
+
+    under = middle_solved[...].reshape(middles * width, columns)
+    group = max(g for g in (1, 2) if tops % g == 0)
+    sent = []
+    for start in range(0, tops, group):
+        total = mul(top_choose[start * width : (start + group) * width], under).astype(BF16)
+        for i in range(group):
+            p = start + i
+            for h in range(2):
+                top_term[h, p] = total[i * width : (i + 1) * width, halves[h]]
+            sent.append(row_start(top_term.at[1 - core, p], top_landed.at[0, p], 0, p, 0))
+
+    def row_sum(k, p):
+        held = top_term[core, p] if k == 0 else top_step[k - 1, p]
+        return held.astype(F32) + top_landed[k, p].astype(F32)
+
+    for k in range(last):
+        for p in range(tops):
+            sent[p].wait_recv()
+            top_step[k, p] = row_sum(k, p).astype(BF16)
+            sent[p] = row_start(top_step.at[k, p], top_landed.at[k + 1, p], k + 1, p, k + 1)
     for p in range(tops):
-        last = row_levels - 1
-        held = top_term[core, p] if last == 0 else top_step[last - 1, p]
-        total = held.astype(F32) + top_landed[last, p].astype(F32)
+        sent[p].wait_recv()
         rhs = top_rhs[p].astype(F32)
         rhs = jnp.where(core == 0, rhs[:, :half], rhs[:, half:])
-        solved = mul(top_inverse[p], (rhs - total).astype(BF16)).astype(BF16)
+        solved = mul(top_inverse[p], (rhs - row_sum(last, p)).astype(BF16)).astype(BF16)
         top_half[core, p] = mul_t(top_inverse[p], solved).astype(BF16)
-    view = top_half.at[core]
-    copy = pltpu.make_async_remote_copy(
-        src_ref=view,
-        dst_ref=view,
-        send_sem=row_send.at[row_levels],
-        recv_sem=row_recv.at[row_levels],
-        device_id=(row_partner[0], me),
-        device_id_type=MESH,
-    )
-    copy.start()
-    pending.append(copy)
-    copy.wait_recv()
+        view = top_half.at[core, p]
+        sent[p] = row_start(view, view, row_levels, p, 0)
     for p in range(tops):
+        sent[p].wait_recv()
         for h in range(2):
             top_out[p, :, halves[h]] = top_half[h, p]
+    stores = [pltpu.make_async_copy(top_out, top_hbm, local_sem.at[5])]
+    stores[0].start()
 
     def middle_backward(k):
         above = top_out[middle_parent[k]]
@@ -287,18 +328,29 @@
     copies = {}
     for h in range(2):
         node_w = (node_solved[h].astype(F32) - mul_t(node_link[0], own[:, halves[h]])).astype(BF16)
-        row_out[me, :, halves[h]] = mul_t(node_inverse[0], node_w).astype(BF16)
-        copies[h, 0, 0] = gather_copy(row_out, down_send, down_recv, h, 0, 0)
-        copies[h, 0, 0].start()
-
-    def middle_store(k, carry):
-        middle_out[k] = middle_backward(k)
-        return carry
-
-    lax.fori_loop(0, middles, middle_store, 0)
-    gather_rest(row_out, down_send, down_recv, copies)
+        node_result = mul_t(node_inverse[0], node_w).astype(BF16)
+        row_out[me, :, halves[h]] = node_result
+        gather_forward(row_out, down_send, down_recv, copies, h, 0, 0)
+        node_out[0, :, halves[h]] = node_result
+
+    def middle_store(ks):
+        w = [(middle_solved[k].astype(F32) - mul_t(middle_link[k], top_out[middle_parent[k]])).astype(BF16) for k in ks]
+        results = [mul_t(middle_inverse[k], w[i]).astype(BF16) for i, k in enumerate(ks)]
+        for i, k in enumerate(ks):
+            middle_out[k] = results[i]
+
+    middle_store(range(middles // 2))
+    for k in range(levels - 1):
+        gather_level(row_out, down_send, down_recv, copies, k)
+    middle_store(range(middles // 2, middles))
+    stores.append(pltpu.make_async_copy(middle_out, middle_hbm, local_sem.at[6]))
+    stores[1].start()
+    gather_level(row_out, down_send, down_recv, copies, levels - 1)
+    pending.extend(copies.values())
     for copy in pending:
         copy.wait_send()
+    for copy in stores:
+        copy.wait()
 
 
 def local(
@@ -323,7 +375,7 @@
     middles, tops = middle_rhs.shape[0], top_rhs.shape[0]
     half = columns // 2
     levels, row_levels = log2(peers), log2(rows)
-    block = max(b for b in (1, 2, 3, 4) if leaves % b == 0)
+    block = max(b for b in (1, 2, 3, 4, 6) if leaves % b == 0)
     steps = leaves // block
     vectors = pl.BlockSpec((block, width, columns), lambda i, t: (i, 0, 0))
     matrices = pl.BlockSpec((block, width, width), lambda i, t: (i, 0, 0))
@@ -348,22 +400,32 @@
     vmem = pl.BlockSpec(memory_space=pltpu.VMEM)
     smem = pl.BlockSpec(memory_space=pltpu.SMEM)
     dma = pltpu.SemaphoreType.DMA
-    row_result, middle_result, top_result = pl.pallas_call(
+    anywhere = pl.BlockSpec(memory_space=pl.ANY)
+    row_result, node_result, middle_result, top_result = pl.pallas_call(
         functools.partial(tree_kernel, rows, peers),
-        in_specs=[vmem] * 4 + [smem] + [vmem] * 3 + [smem] + [vmem] * 2,
-        out_specs=[vmem] * 3,
+        in_specs=[vmem] * 4 + [smem] + [anywhere] * 3 + [smem] + [anywhere] * 2,
+        out_specs=[vmem] * 2 + [anywhere] * 2,
         out_shape=[
             jax.ShapeDtypeStruct((peers, width, columns), BF16),
+            jax.ShapeDtypeStruct(node_rhs.shape, BF16),
             jax.ShapeDtypeStruct(middle_rhs.shape, BF16),
             jax.ShapeDtypeStruct(top_rhs.shape, BF16),
         ],
         scratch_shapes=[
+            pltpu.VMEM(middle_rhs.shape, BF16),
+            pltpu.VMEM(middle_inverse.shape, BF16),
+            pltpu.VMEM(middle_link.shape, BF16),
+            pltpu.VMEM(top_rhs.shape, BF16),
+            pltpu.VMEM(top_inverse.shape, BF16),
+            pltpu.VMEM(middle_rhs.shape, BF16),
+            pltpu.VMEM(top_rhs.shape, BF16),
+            dma((7,)),
             pltpu.VMEM((peers, width, columns), BF16),
             pltpu.VMEM((2, peers - 1, width, half), BF16),
             pltpu.VMEM((peers, width, columns), BF16),
-            pltpu.VMEM((middles, width, peers * width), BF16),
+            pltpu.VMEM((middles * width, peers * width), BF16),
             pltpu.VMEM((middles, width, columns), BF16),
-            pltpu.VMEM((tops, width, middles * width), BF16),
+            pltpu.VMEM((tops * width, middles * width), BF16),
             pltpu.VMEM((2, tops, width, half), BF16),
             pltpu.VMEM((row_levels, tops, width, half), BF16),
             pltpu.VMEM((row_levels, tops, width, half), BF16),
@@ -374,8 +436,8 @@
             dma((2, peers - 1)),
             dma((2, peers - 1)),
             dma((2, peers - 1)),
-            dma((row_levels + 1,)),
-            dma((row_levels + 1,)),
+            dma((row_levels + 1, tops)),
+            dma((row_levels + 1, tops)),
         ],
         compiler_params=pltpu.CompilerParams(
             collective_id=0, has_side_effects=True, vmem_limit_bytes=VMEM_LIMIT
@@ -394,20 +456,20 @@
         top_rhs,
         top_inverse,
     )
-    node_result = lax.dynamic_slice_in_dim(row_result, lax.axis_index("col"), 1)
-
-    leaf_result = pl.pallas_call(
-        functools.partial(leaf_backward_kernel, block, peers),
+
+    leaf_result, node_result, middle_result, top_result = pl.pallas_call(
+        functools.partial(leaf_backward_kernel, steps, block, peers),
         grid_spec=pltpu.PrefetchScalarGridSpec(
             num_scalar_prefetch=1,
             grid=(steps,),
-            in_specs=[vectors, matrices, matrices, slots],
-            out_specs=vectors,
+            in_specs=[vectors, matrices, matrices, slots] + [anywhere] * 3,
+            out_specs=[vectors] + [anywhere] * 3,
+            scratch_shapes=[dma((3,))],
         ),
-        out_shape=jax.ShapeDtypeStruct(leaf_rhs.shape, BF16),
+        out_shape=[jax.ShapeDtypeStruct(a.shape, BF16) for a in (leaf_rhs, node_rhs, middle_rhs, top_rhs)],
         compiler_params=pltpu.CompilerParams(vmem_limit_bytes=VMEM_LIMIT),
         name="leaf_backward",
-    )(leaf_parent, leaf_solved, leaf_inverse, leaf_link, row_result)
+    )(leaf_parent, leaf_solved, leaf_inverse, leaf_link, row_result, node_result, middle_result, top_result)
     return (leaf_result, node_result, middle_result, top_result)
 
 

time: 92.3 us -> 129 us (1.40)
  Pallas kernels: 87.8 us -> 128 us
  local copies, waits for them, and re-layouts: 3.34 us -> 0 us
    pallas_call x1, Pallas kernels: 9.72 us -> 56 us  [local(): pl.pallas_call(functools.partial(leaf_backward_kernel, steps, block, peer...]
    pallas_call x1, Pallas kernels: 68.4 us -> 64.8 us  [local(): pl.pallas_call(functools.partial(tree_kernel, rows, peers), in_specs=[vme...]
    pallas_call x1, Pallas kernels: 9.66 us -> 6.88 us  [local(): pl.pallas_call(functools.partial(leaf_forward_kernel, steps, block, peers...]
    unnamed x6 -> x0, local copies, waits for them, and re-layouts: 1.77 us -> none
    dynamic_slice x1 -> x0, local copies, waits for them, and re-layouts: 1.57 us -> none  [local(): node_result = lax.dynamic_slice_in_dim(row_result, lax.axis_index('col'), 1)]
where the time goes in v2:
time: 129 us; the launch traced here: 128 us
  Pallas kernels  128 us (99%)
    pallas_call x1, Pallas kernels, local(): pl.pallas_call(functools.partial(tree_kernel, rows, peers), in_specs=[vme...  64.8 us
    pallas_call x1, Pallas kernels, local(): pl.pallas_call(functools.partial(leaf_backward_kernel, steps, block, peer...  56 us
    pallas_call x1, Pallas kernels, local(): pl.pallas_call(functools.partial(leaf_forward_kernel, steps, block, peers...  6.88 us

profile of v2, /device:TPU:0, one launch (start us, length us, event | category | flops | bytes accessed | tf_op | source)
XLA Modules:
  0.0 128.4 jit_solution(7046243875064075401)
XLA Ops:
  0.6 6.9 %leaf_forward.1 = (bf16[24,128,512]{2,1,0:T(8,128)(2,1)}, bf16[8,128,512]{2,1,0:T(8,128)(2,1)}) custom-call(s32[24]{0:T(128)} %target.3, bf16[24,128,512]{2,1,0:T(8,128)(2,1)} %rhs.1, bf16[24,128,128]{2,1,0:T(8,128)(2,1)} %inverse.3, bf16[24,128,128]{2,1,0:T(8,128)(2,1)} %link.3), custom_call_target="tpu_custom_call" | custom-call | tf_op jit(solution)/shard_map/leaf_forward/pallas_call | solution.py:383
  7.5 64.8 %tree.1 = (bf16[8,128,512]{2,1,0:T(8,128)(2,1)}, bf16[1,128,512]{2,1,0:T(8,128)(2,1)}, bf16[8,128,512]{2,1,0:T(8,128)(2,1)}, bf16[4,128,512]{2,1,0:T(8,128)(2,1)}) custom-call(bf16[8,128,512]{2,1,0:T(8,128)(2,1)} %get-tuple-element.11.part, bf16[1,128,512]{2,1,0:T(8,128)(2,1)} %node_rhs.1, bf16[1,128,128]{2,1,0:T(8,128)(2,1)} %node_inverse.1, ...), custom_call_target="tpu_custom_call" | custom-call | tf_op jit(solution)/shard_map/tree/pallas_call | solution.py:404
  72.4 56.0 %leaf_backward.1 = (bf16[24,128,512]{2,1,0:T(8,128)(2,1)}, bf16[1,128,512]{2,1,0:T(8,128)(2,1)}, bf16[8,128,512]{2,1,0:T(8,128)(2,1)}, bf16[4,128,512]{2,1,0:T(8,128)(2,1)}) custom-call(s32[24]{0:T(128)} %target.3, bf16[24,128,512]{2,1,0:T(8,128)(2,1)} %get-tuple-element.10.solved, bf16[24,128,128]{2,1,0:T(8,128)(2,1)} %inverse.3, ...), custom_call_target="tpu_custom_call" | custom-call | tf_op jit(solution)/shard_map/leaf_backward/pallas_call | solution.py:460

commit v3 on v2

--- a/solution.py
+++ b/solution.py
@@ -42,28 +42,21 @@
 
 
 def leaf_backward_kernel(
-    steps, block, peers, target, solved, inverse, link, above, node, middle, top, result, node_out, middle_out, top_out, sem
+    steps, block, peers, target, solved, inverse, link, above, node, middle, top, result, node_out, middle_out, top_out
 ):
     step = pl.program_id(0)
-    pairs = [(node, node_out), (middle, middle_out), (top, top_out)]
-    passed = [pltpu.make_async_copy(src, dst, sem.at[i]) for i, (src, dst) in enumerate(pairs)]
+    middle_out[...] = middle[...]
+    top_out[...] = top[...]
 
     @pl.when(step == 0)
     def _():
-        for copy in passed:
-            copy.start()
+        node_out[...] = node[...]
 
     parents = [above[target[step * block + i] % peers] for i in range(block)]
     w = [(solved[i].astype(F32) - mul_t(link[i], parents[i])).astype(BF16) for i in range(block)]
     results = [mul_t(inverse[i], w[i]).astype(BF16) for i in range(block)]
     for i in range(block):
         result[i] = results[i]
-
-    @pl.when(step == steps - 1)
-    def _():
-        for copy in passed:
-            copy.wait()
-
 
 def bits_of(index, count):
     return [(index // (1 << b)) % 2 for b in range(count)]
@@ -457,14 +450,19 @@
         top_inverse,
     )
 
+    passed = []
+    for count in (1, middles, tops):
+        if count % steps == 0:
+            passed.append(pl.BlockSpec((count // steps, width, columns), lambda i, t: (i, 0, 0)))
+        else:
+            passed.append(pl.BlockSpec((count, width, columns), lambda i, t: (0, 0, 0)))
     leaf_result, node_result, middle_result, top_result = pl.pallas_call(
         functools.partial(leaf_backward_kernel, steps, block, peers),
         grid_spec=pltpu.PrefetchScalarGridSpec(
             num_scalar_prefetch=1,
             grid=(steps,),
-            in_specs=[vectors, matrices, matrices, slots] + [anywhere] * 3,
-            out_specs=[vectors] + [anywhere] * 3,
-            scratch_shapes=[dma((3,))],
+            in_specs=[vectors, matrices, matrices, slots] + passed,
+            out_specs=[vectors] + passed,
         ),
         out_shape=[jax.ShapeDtypeStruct(a.shape, BF16) for a in (leaf_rhs, node_rhs, middle_rhs, top_rhs)],
         compiler_params=pltpu.CompilerParams(vmem_limit_bytes=VMEM_LIMIT),

time: 129 us -> 80.4 us (0.62)
  Pallas kernels: 128 us -> 79.5 us
    pallas_call x1, Pallas kernels: 56 us -> 7.76 us  [local(): pl.pallas_call(functools.partial(leaf_backward_kernel, steps, block, peer...]
where the time goes in v3:
time: 80.4 us; the launch traced here: 80.1 us
  Pallas kernels  79.5 us (99%)
    pallas_call x1, Pallas kernels, local(): pl.pallas_call(functools.partial(tree_kernel, rows, peers), in_specs=[vme...  64.8 us
    pallas_call x1, Pallas kernels, local(): pl.pallas_call(functools.partial(leaf_backward_kernel, steps, block, peer...  7.76 us
    pallas_call x1, Pallas kernels, local(): pl.pallas_call(functools.partial(leaf_forward_kernel, steps, block, peers...  6.88 us

profile of v3, /device:TPU:0, one launch (start us, length us, event | category | flops | bytes accessed | tf_op | source)
XLA Modules:
  0.0 80.1 jit_solution(12288912248786945229)
XLA Ops:
  0.6 6.9 %leaf_forward.1 = (bf16[24,128,512]{2,1,0:T(8,128)(2,1)}, bf16[8,128,512]{2,1,0:T(8,128)(2,1)}) custom-call(s32[24]{0:T(128)} %target.3, bf16[24,128,512]{2,1,0:T(8,128)(2,1)} %rhs.1, bf16[24,128,128]{2,1,0:T(8,128)(2,1)} %inverse.3, bf16[24,128,128]{2,1,0:T(8,128)(2,1)} %link.3), custom_call_target="tpu_custom_call" | custom-call | tf_op jit(solution)/shard_map/leaf_forward/pallas_call | solution.py:376
  7.5 64.8 %tree.1 = (bf16[8,128,512]{2,1,0:T(8,128)(2,1)}, bf16[1,128,512]{2,1,0:T(8,128)(2,1)}, bf16[8,128,512]{2,1,0:T(8,128)(2,1)}, bf16[4,128,512]{2,1,0:T(8,128)(2,1)}) custom-call(bf16[8,128,512]{2,1,0:T(8,128)(2,1)} %get-tuple-element.11.part, bf16[1,128,512]{2,1,0:T(8,128)(2,1)} %node_rhs.1, bf16[1,128,128]{2,1,0:T(8,128)(2,1)} %node_inverse.1, ...), custom_call_target="tpu_custom_call" | custom-call | tf_op jit(solution)/shard_map/tree/pallas_call | solution.py:397
  72.4 7.8 %leaf_backward.1 = (bf16[24,128,512]{2,1,0:T(8,128)(2,1)}, bf16[1,128,512]{2,1,0:T(8,128)(2,1)}, bf16[8,128,512]{2,1,0:T(8,128)(2,1)}, bf16[4,128,512]{2,1,0:T(8,128)(2,1)}) custom-call(s32[24]{0:T(128)} %target.3, bf16[24,128,512]{2,1,0:T(8,128)(2,1)} %get-tuple-element.10.solved, bf16[24,128,128]{2,1,0:T(8,128)(2,1)} %inverse.3, ...), custom_call_target="tpu_custom_call" | custom-call | tf_op jit(solution)/shard_map/leaf_backward/pallas_call | solution.py:459

commit v4 on v3

--- a/solution.py
+++ b/solution.py
@@ -114,6 +114,8 @@
     row, me = lax.axis_index("row"), lax.axis_index("col")
     width, columns = node_rhs.shape[1:]
     half = columns // 2
+    cut = columns * 3 // 4
+    cuts = [slice(0, cut), slice(cut, columns)]
     halves = [slice(0, half), slice(half, columns)]
     middles, tops = middle_rhs.shape[0], top_rhs.shape[0]
     levels, row_levels = log2(peers), log2(rows)
@@ -157,8 +159,8 @@
         place = scatter_place(k, j)
         source = part if k == 0 else work
         copy = pltpu.make_async_remote_copy(
-            src_ref=source.at[slot, :, halves[h]],
-            dst_ref=landed.at[h, place],
+            src_ref=source.at[slot, :, cuts[h]],
+            dst_ref=landed.at[place, :, cuts[h]],
             send_sem=rs_send.at[h, place],
             recv_sem=rs_recv.at[h, place],
             device_id=(row, partner[orders[h][k]]),
@@ -172,7 +174,7 @@
         scatter[h, k, j].wait_recv()
         slot = scatter_slot(h, k, j, 0)
         source = part if k == 0 else work
-        return slot, source[slot, :, halves[h]].astype(F32) + landed[h, scatter_place(k, j)].astype(F32)
+        return slot, source[slot, :, cuts[h]].astype(F32) + landed[scatter_place(k, j), :, cuts[h]].astype(F32)
 
     for j in reversed(range(1 << (levels - 1))):
         for h in range(2):
@@ -205,7 +207,7 @@
         for j in reversed(range(2 * count)):
             for h in range(2):
                 slot, value = scatter_add(h, k - 1, j)
-                work[slot, :, halves[h]] = value.astype(BF16)
+                work[slot, :, cuts[h]] = value.astype(BF16)
                 if j >= count:
                     scatter_start(h, k, j - count)
 
@@ -217,7 +219,7 @@
         order = orders[h][::-1]
         slot = gather_slot(h, order[:k], j)
         place = (1 << k) - 1 + j
-        view = buffer.at[slot, :, halves[h]]
+        view = buffer.at[slot, :, cuts[h]]
         return pltpu.make_async_remote_copy(
             src_ref=view,
             dst_ref=view,
@@ -243,9 +245,9 @@
     node_solved = []
     for h in range(2):
         _, total = scatter_add(h, levels - 1, 0)
-        node_y = (node_rhs[0, :, halves[h]].astype(F32) - total).astype(BF16)
+        node_y = (node_rhs[0, :, cuts[h]].astype(F32) - total).astype(BF16)
         solved = mul(node_inverse[0], node_y).astype(BF16)
-        updates[me, :, halves[h]] = mul(node_link[0], solved).astype(BF16)
+        updates[me, :, cuts[h]] = mul(node_link[0], solved).astype(BF16)
         gather_forward(updates, up_send, up_recv, copies, h, 0, 0)
         node_solved.append(solved)
     for k in range(levels):
@@ -320,11 +322,11 @@
     own = middle_backward(node_parent[me] % middles)
     copies = {}
     for h in range(2):
-        node_w = (node_solved[h].astype(F32) - mul_t(node_link[0], own[:, halves[h]])).astype(BF16)
+        node_w = (node_solved[h].astype(F32) - mul_t(node_link[0], own[:, cuts[h]])).astype(BF16)
         node_result = mul_t(node_inverse[0], node_w).astype(BF16)
-        row_out[me, :, halves[h]] = node_result
+        row_out[me, :, cuts[h]] = node_result
         gather_forward(row_out, down_send, down_recv, copies, h, 0, 0)
-        node_out[0, :, halves[h]] = node_result
+        node_out[0, :, cuts[h]] = node_result
 
     def middle_store(ks):
         w = [(middle_solved[k].astype(F32) - mul_t(middle_link[k], top_out[middle_parent[k]])).astype(BF16) for k in ks]
@@ -414,7 +416,7 @@
             pltpu.VMEM(top_rhs.shape, BF16),
             dma((7,)),
             pltpu.VMEM((peers, width, columns), BF16),
-            pltpu.VMEM((2, peers - 1, width, half), BF16),
+            pltpu.VMEM((peers - 1, width, columns), BF16),
             pltpu.VMEM((peers, width, columns), BF16),
             pltpu.VMEM((middles * width, peers * width), BF16),
             pltpu.VMEM((middles, width, columns), BF16),

time: 80.4 us -> 83.2 us (1.035)
  Pallas kernels: 79.5 us -> 82.3 us
    pallas_call x1, Pallas kernels: 64.8 us -> 67.6 us  [local(): pl.pallas_call(functools.partial(tree_kernel, rows, peers), in_specs=[vme...]
where the time goes in v4:
time: 83.2 us; the launch traced here: 82.9 us
  Pallas kernels  82.3 us (99%)
    pallas_call x1, Pallas kernels, local(): pl.pallas_call(functools.partial(tree_kernel, rows, peers), in_specs=[vme...  67.6 us
    pallas_call x1, Pallas kernels, local(): pl.pallas_call(functools.partial(leaf_backward_kernel, steps, block, peer...  7.76 us
    pallas_call x1, Pallas kernels, local(): pl.pallas_call(functools.partial(leaf_forward_kernel, steps, block, peers...  6.88 us

profile of v4, /device:TPU:0, one launch (start us, length us, event | category | flops | bytes accessed | tf_op | source)
XLA Modules:
  0.0 82.9 jit_solution(4495899031687003992)
XLA Ops:
  0.6 6.9 %leaf_forward.1 = (bf16[24,128,512]{2,1,0:T(8,128)(2,1)}, bf16[8,128,512]{2,1,0:T(8,128)(2,1)}) custom-call(s32[24]{0:T(128)} %target.3, bf16[24,128,512]{2,1,0:T(8,128)(2,1)} %rhs.1, bf16[24,128,128]{2,1,0:T(8,128)(2,1)} %inverse.3, bf16[24,128,128]{2,1,0:T(8,128)(2,1)} %link.3), custom_call_target="tpu_custom_call" | custom-call | tf_op jit(solution)/shard_map/leaf_forward/pallas_call | solution.py:378
  7.5 67.6 %tree.1 = (bf16[8,128,512]{2,1,0:T(8,128)(2,1)}, bf16[1,128,512]{2,1,0:T(8,128)(2,1)}, bf16[8,128,512]{2,1,0:T(8,128)(2,1)}, bf16[4,128,512]{2,1,0:T(8,128)(2,1)}) custom-call(bf16[8,128,512]{2,1,0:T(8,128)(2,1)} %get-tuple-element.11.part, bf16[1,128,512]{2,1,0:T(8,128)(2,1)} %node_rhs.1, bf16[1,128,128]{2,1,0:T(8,128)(2,1)} %node_inverse.1, ...), custom_call_target="tpu_custom_call" | custom-call | tf_op jit(solution)/shard_map/tree/pallas_call | solution.py:399
  75.1 7.8 %leaf_backward.1 = (bf16[24,128,512]{2,1,0:T(8,128)(2,1)}, bf16[1,128,512]{2,1,0:T(8,128)(2,1)}, bf16[8,128,512]{2,1,0:T(8,128)(2,1)}, bf16[4,128,512]{2,1,0:T(8,128)(2,1)}) custom-call(s32[24]{0:T(128)} %target.3, bf16[24,128,512]{2,1,0:T(8,128)(2,1)} %get-tuple-element.10.solved, bf16[24,128,128]{2,1,0:T(8,128)(2,1)} %inverse.3, ...), custom_call_target="tpu_custom_call" | custom-call | tf_op jit(solution)/shard_map/leaf_backward/pallas_call | solution.py:461
